TPU v7x, 512 devices: a whole 4x4x16 slice. The times are simulated.
512 devices in a mesh: region: 128 (over z, y, core), coarse: 4 (over x).
Axes of the slice: x: 4, y: 4, z: 16, core: 2. Of those that a mesh axis runs over, the one named last changes fastest.
Arguments:
- source_jump: float32 [512, 768, 256], P(('region', 'coarse')), may hold values from -6 to 6
- neumann_inverse: bfloat16 [512, 768, 768], P(('region', 'coarse')), may hold values from -1 to 2, as said below
- dirichlet_schur: bfloat16 [512, 768, 768], P(('region', 'coarse')), may hold values from -10 to 20, as said below
- corner_coupling: float32 [512, 4, 768], P(('region', 'coarse')), may hold values from -0.21875 to 0.21875
- corner_map: int32 [512, 4], P(('region', 'coarse')), may hold values from 0 to 515, as said below
- face_map: int32 [512, 2, 192], P(('region', 'coarse')), may hold values from 0 to 191, each once within a row
- coarse_inverse: float32 [516, 516], P('coarse'), may hold values from -1 to 2, as said below
Outputs:
- multiplier: float32 [512, 768, 256], P(('region', 'coarse'))
- residual: float32 [512, 768, 256], P(('region', 'coarse'))
Inputs may be any that keep to these rules, and one draw needn't show every extreme that they name: `corner_map`: subdomain (a, b) names, in an order of its own, the coarse unknowns of the four grid vertices (a or a+1, b or b+1 mod 4) that its vertical edges stand on; the unknowns of vertices (a', 0) to (a', 4 - 1) are a' 4 to a' 4 + 4 - 1 in some order. `face_map`: each row of each face is a permutation. `neumann_inverse`: each subdomain's matrix is symmetric positive definite. `dirichlet_schur`: each subdomain's matrix is symmetric positive definite. `coarse_inverse`: symmetric positive definite.
All inputs are finite; a program needn't handle non-finite values.
Results may differ from a plain program's by a relative error of at most 0.0051.
Values sent between devices are 32-bit elements; how exact they have to be, the bound alone decides.
A program may use at most 64 MiB of HBM per device.

v0:
```python
import jax
import jax.numpy as jnp
from jax import lax
from jax.sharding import PartitionSpec as P

ITERS = 3


def extended(value, sides, width, wrap):
    for axis, dim in sides:
        devices, length = (lax.axis_size(axis), value.shape[dim])
        up = [(i, (i + 1) % devices) for i in range(devices if wrap else devices - 1)]
        down = [(j, i) for i, j in up]
        last = lax.slice_in_dim(value, length - width, length, axis=dim)
        initial = lax.slice_in_dim(value, 0, width, axis=dim)
        before = lax.ppermute(last, axis, up)
        after = lax.ppermute(initial, axis, down)
        value = jnp.concatenate([before, value, after], axis=dim)
    return value


def dual_jump(field, forward, backward):
    faces = field[0].reshape(4, -1, field.shape[2])
    along_region = jnp.stack([faces[0], jnp.take(faces[1], backward[0], axis=0)])
    region_pad = extended(along_region, (("region", 0),), 1, False)
    along_coarse = jnp.stack([faces[2], jnp.take(faces[3], backward[1], axis=0)])
    coarse_pad = extended(along_coarse, (("coarse", 0),), 1, True)
    position = lax.axis_index("region")
    region_count = lax.axis_size("region")
    first = jnp.where(position > 0, faces[0] - region_pad[0], 0.0)
    second = jnp.where(
        position < region_count - 1, faces[1] - jnp.take(region_pad[3], forward[0], axis=0), 0.0
    )
    third = faces[2] - coarse_pad[0]
    fourth = faces[3] - jnp.take(coarse_pad[3], forward[1], axis=0)
    return jnp.stack([first, second, third, fourth]).reshape(field.shape)


def coarse_solve(scattered, coarse_inverse):
    totals = lax.psum(scattered, ("region", "coarse"))
    owned = jnp.dot(coarse_inverse, totals, precision=lax.Precision.HIGHEST)
    return lax.all_gather(owned, "coarse", axis=0, tiled=True)


def neumann_apply(
    direction, neumann_inverse, corner_coupling, onehot, coarse_inverse, forward, backward
):
    local = jnp.dot(
        neumann_inverse[0], direction[0].astype(jnp.bfloat16), preferred_element_type=jnp.float32
    )
    corner_load = jnp.dot(corner_coupling[0], direction[0], precision=lax.Precision.HIGHEST)
    scattered = jnp.einsum("ca,ck->ak", onehot, corner_load, precision=lax.Precision.HIGHEST)
    values = coarse_solve(scattered, coarse_inverse)
    corner_values = jnp.dot(onehot, values, precision=lax.Precision.HIGHEST)
    field = (
        local
        + jnp.einsum(
            "cm,ck->mk", corner_coupling[0], corner_values, precision=lax.Precision.HIGHEST
        )
    )[None]
    image = dual_jump(field, forward, backward)
    local_sum = jnp.sum(direction[0] * image[0], axis=0)
    return (image, lax.psum(local_sum, ("region", "coarse")))


def precond_apply(residual, dirichlet_schur, forward, backward):
    scaled = (0.5 * residual[0]).astype(jnp.bfloat16)
    weighted = jnp.dot(dirichlet_schur[0], scaled, preferred_element_type=jnp.float32)[None]
    precond = 0.5 * dual_jump(weighted, forward, backward)
    local_sum = jnp.sum(residual[0] * precond[0], axis=0)
    return (precond, lax.psum(local_sum, ("region", "coarse")))


def body(
    source_jump,
    neumann_inverse,
    dirichlet_schur,
    corner_coupling,
    corner_map,
    face_map,
    coarse_inverse,
):
    forward = face_map[0]
    backward = jnp.argsort(forward, axis=1)
    coarse_total = coarse_inverse.shape[1]
    onehot = (corner_map[0][:, None] == jnp.arange(coarse_total, dtype=jnp.int32)[None, :]).astype(
        jnp.float32
    )
    residual = dual_jump(source_jump, forward, backward)
    multiplier = jnp.zeros_like(residual)
    precond, precond_sum = precond_apply(residual, dirichlet_schur, forward, backward)
    direction = precond
    for iteration in range(ITERS):
        image, curve_sum = neumann_apply(
            direction, neumann_inverse, corner_coupling, onehot, coarse_inverse, forward, backward
        )
        step_len = precond_sum / curve_sum
        multiplier = multiplier + step_len * direction
        residual = residual - step_len * image
        if iteration + 1 < ITERS:
            precond, next_sum = precond_apply(residual, dirichlet_schur, forward, backward)
            direction = precond + next_sum / precond_sum * direction
            precond_sum = next_sum
    return (multiplier, residual)


def solution(mesh):
    placed = (
        P(("region", "coarse"), None, None),
        P(("region", "coarse"), None, None),
        P(("region", "coarse"), None, None),
        P(("region", "coarse"), None, None),
        P(("region", "coarse"), None),
        P(("region", "coarse"), None, None),
        P("coarse", None),
    )
    return jax.shard_map(
        body,
        mesh=mesh,
        in_specs=placed,
        out_specs=(P(("region", "coarse"), None, None), P(("region", "coarse"), None, None)),
        check_vma=False,
    )
```

profile of v0, /device:TPU:1, one launch (start us, length us, event | category | flops | bytes accessed | tf_op | source)
XLA Modules:
  0.0 2188.4 jit_solution(4139578136656369146)
XLA Ops:
  7.2 4.0 sort.17
  13.4 4.1 collective-permute-start.2
  18.5 4.0 collective-permute-start
  25.6 5.5 collective-permute-start.1
  34.0 5.7 collective-permute-done.3
  61.6 4.4 collective-permute-done.6
  71.0 464.9 %all-reduce.5.cloned.1.call-done = f32[516,256]{1,0:T(8,128)} async-done(((f32[516,256]{1,0:T(8,128)}), f32[516,256]{1,0:T(8,128)}) %all-reduce.5.cloned.1.call-update) | async-done | bytes 528400 | tf_op jit(solution)/shard_map/psum | solution.py:40
  537.6 10.8 all-gather
  549.7 7.2 collective-permute-start.9
  582.4 103.3 %all-reduce = (f32[256]{0:T(256)S(1)}, f32[256]{0:T(256)S(1)}) all-reduce(f32[256]{0:T(256)S(1)} %get-tuple-element.6, f32[256]{0:T(256)S(1)} %get-tuple-element.5), channel_id=1, replica_groups=mesh['region'=128,'coarse'=4] {'region','coarse'}, use_global_device_ids=true, to_apply=%region_2.4 | all-reduce | flops 512 | bytes 4096 | tf_op jit(solution)/shard_map/psum | solution.py:71
  709.9 4.9 collective-permute-done.14
  715.9 103.3 %psum.66 = f32[256]{0:T(256)S(1)} all-reduce(f32[256]{0:T(256)S(1)} %get-tuple-element.34), channel_id=1, replica_groups=mesh['region'=128,'coarse'=4] {'region','coarse'}, use_global_device_ids=true, to_apply=%region_7.9 | all-reduce | flops 256 | bytes 2048 | tf_op jit(solution)/shard_map/psum | solution.py:71
  826.0 449.9 %all-reduce.7.cloned.1.call-done = f32[516,256]{1,0:T(8,128)} async-done(((f32[516,256]{1,0:T(8,128)}), f32[516,256]{1,0:T(8,128)}) %all-reduce.7.cloned.1.call-update) | async-done | bytes 528400 | tf_op jit(solution)/shard_map/psum | solution.py:40
  1277.6 12.3 all-gather.1
  1294.0 6.2 collective-permute-start.17
  1319.4 4.0 collective-permute-start.16
  1329.4 102.6 %psum.68 = f32[256]{0:T(256)} all-reduce(f32[256]{0:T(256)} %get-tuple-element.21), channel_id=1, replica_groups=mesh['region'=128,'coarse'=4] {'region','coarse'}, use_global_device_ids=true, to_apply=%region_10.12 | all-reduce | flops 256 | bytes 2048 | tf_op jit(solution)/shard_map/psum | solution.py:63
  1460.3 4.8 collective-permute-done.22
  1467.7 103.6 %psum.69 = f32[256]{0:T(256)S(1)} all-reduce(f32[256]{0:T(256)} %multiply_reduce_fusion.1), channel_id=1, replica_groups=mesh['region'=128,'coarse'=4] {'region','coarse'}, use_global_device_ids=true, to_apply=%region_12.14 | all-reduce | flops 256 | bytes 2048 | tf_op jit(solution)/shard_map/psum | solution.py:71
  1579.3 449.3 %all-reduce.9.cloned.1.call-done = f32[516,256]{1,0:T(8,128)} async-done(((f32[516,256]{1,0:T(8,128)}), f32[516,256]{1,0:T(8,128)}) %all-reduce.9.cloned.1.call-update) | async-done | bytes 528400 | tf_op jit(solution)/shard_map/psum | solution.py:40
  2030.2 10.9 all-gather.2
  2044.2 7.2 collective-permute-start.25
  2066.4 4.0 collective-permute-start.24
  2075.2 102.9 %psum.71 = f32[256]{0:T(256)S(1)} all-reduce(f32[256]{0:T(256)} %get-tuple-element.23), channel_id=1, replica_groups=mesh['region'=128,'coarse'=4] {'region','coarse'}, use_global_device_ids=true, to_apply=%region_15.17 | all-reduce | flops 256 | bytes 2048 | tf_op jit(solution)/shard_map/psum | solution.py:63
  (324 shorter events, 193.1 us)
Async XLA Ops:
  7.2 528.8 %all-reduce.5.cloned.1.call-start = ((), (), s32[]{:S(2)}) async-start(), calls=%async_computation | async-start | bytes 1064960 | tf_op jit(solution)/shard_map/psum | solution.py:40
  13.4 9.3 collective-permute-start.2
  25.6 7.5 collective-permute-start.1
  31.2 8.5 collective-permute-start.3
  44.5 8.5 collective-permute-start.7
  56.8 9.2 collective-permute-start.6
  69.5 1206.4 %all-reduce.7.cloned.1.call-start = ((), (), s32[]{:S(2)}) async-start(), calls=%async_computation.1 | async-start | bytes 1064960 | tf_op jit(solution)/shard_map/psum | solution.py:40
  549.7 11.7 collective-permute-start.9
  556.9 8.5 collective-permute-start.11
  572.1 9.2 collective-permute-start.10
  690.8 8.5 collective-permute-start.15
  704.7 10.0 collective-permute-start.14
  707.4 7.4 collective-permute-start.12
  824.1 1204.5 %all-reduce.9.cloned.1.call-start = ((), (), s32[]{:S(2)}) async-start(), calls=%async_computation.2 | async-start | bytes 1064960 | tf_op jit(solution)/shard_map/psum | solution.py:40
  1294.0 10.7 collective-permute-start.17
  1300.3 8.5 collective-permute-start.19
  1316.9 9.9 collective-permute-start.18
  1319.4 7.4 collective-permute-start.16
  1436.7 8.7 collective-permute-start.23
  1455.3 9.8 collective-permute-start.22
  1457.7 7.4 collective-permute-start.20
  2044.2 11.7 collective-permute-start.25
  2051.4 8.5 collective-permute-start.27
  2064.2 9.3 collective-permute-start.26
  (85 other events, 3313.0 us)
Sparse Core Ops, SparseCore 0:
  69.6 466.2 all-reduce.4
  824.2 451.6 all-reduce.6
  1577.0 451.5 all-reduce.8
where the time goes:
time: 2190 us
  waiting for transfers between devices  1420 us (65%)
  blocking collectives  550 us (25%)
  starting transfers between devices  97.5 us (4%)
  other arithmetic  42.1 us (2%)
  local copies, waits for them, and re-layouts  40.7 us (2%)
  matrix products  23 us (1%)
    psum x3, waiting for transfers between devices, coarse_solve(): totals = lax.psum(scattered, ('region', 'coarse'))  1360 us
    psum x3, blocking collectives, precond_apply(): return (precond, lax.psum(local_sum, ('region', 'coarse')))  310 us
    psum x2, blocking collectives, neumann_apply(): return (image, lax.psum(local_sum, ('region', 'coarse')))  206 us
    ppermute x14, starting transfers between devices, extended(): after = lax.ppermute(initial, axis, down)  55.9 us
  transfers between devices with their start and end apart: 31, of which 23 were waited for; matrix products, arithmetic and copies ran while one was open for 1% of the time, Pallas kernels for 0%

commit v1 on v0

v1 whole, which is shorter than its diff:
```python
import functools

import jax
import jax.numpy as jnp
from jax import lax
from jax.experimental import pallas as pl
from jax.experimental.pallas import tpu as pltpu
from jax.sharding import PartitionSpec as P

ITERS = 3
MESH = pl.DeviceIdType.MESH
F32, BF16 = jnp.float32, jnp.bfloat16

PLANE = 8
NX = 4
GROUP = PLANE * NX
NZ = 16
FACE = 192
M = 4 * FACE
K = 256
BASE = NX * PLANE
USED = NX * (PLANE + 3)
WIDE = 640


def rounded(value):
    return value.astype(BF16).astype(F32)


def dot(a, b):
    return jnp.dot(a, b, preferred_element_type=F32)


def dot_nt(a, b):
    return lax.dot_general(a, b, (((1,), (1,)), ((), ())), preferred_element_type=F32)


def permuted(onehot, value):
    high = value.astype(BF16)
    rest = value - high.astype(F32)
    middle = rest.astype(BF16)
    low = (rest - middle.astype(F32)).astype(BF16)
    return (dot(onehot, high) + dot(onehot, middle)) + dot(onehot, low)


def kernel(
    source, neumann, dirichlet, coupling, corner_map, face_map, coarse_inverse,
    x_out, r_out,
    residual, solved, search, image, weighted, dual, local,
    weighted_in, local_in, corner_out, corner_in, frame,
    perms, dirichlet_all, neumann_own, raw_dirichlet, raw_neumann, spread,
    blocks, assembled, inverse_high, inverse_low, shifted, scalars,
    loads_out, loads_in, plane_loads, all_loads, dots_out, all_dots, back_out, back_in,
    fetch_sem, face_send, source_recv, weighted_recv, local_recv, corner_send, corner_recv,
    block_send, block_recv, core_send, core_recv,
    group_send, loads_recv, plane_send, all_recv, dots_send, dots_recv, back_send, back_recv,
):
    region, coarse = lax.axis_index("region"), lax.axis_index("coarse")
    z, place = lax.div(region, PLANE), lax.rem(region, PLANE)
    core = lax.rem(region, 2)
    own = place * NX + coarse
    n_region = NZ * PLANE
    left = (lax.rem(region + n_region - 1, n_region), coarse)
    right = (lax.rem(region + 1, n_region), coarse)
    before = (region, lax.rem(coarse + NX - 1, NX))
    after = (region, lax.rem(coarse + 1, NX))
    neighbours = (left, right, before, after)
    partner_face = (1, 0, 3, 2)
    paired = (region > 0, region < n_region - 1, None, None)

    def in_group(step):
        peer = lax.rem(own + step, GROUP)
        return peer, (z * PLANE + lax.div(peer, NX), lax.rem(peer, NX))

    def along_z(step):
        return (lax.rem(z + step, NZ) * PLANE + place, coarse)

    def rows(face):
        return pl.ds(face * FACE, FACE)

    def remote(src, dst, send, recv, device):
        return pltpu.make_async_remote_copy(
            src_ref=src, dst_ref=dst, send_sem=send, recv_sem=recv, device_id=device, device_id_type=MESH
        )

    def drain(ref, sem):
        pltpu.make_async_copy(ref, ref, sem).wait()

    def send_faces(src, dst, send, recv):
        copies = [None] * 4
        for face in range(4):
            there = partner_face[face]
            copy = remote(
                src.at[rows(face)], dst.at[rows(there)], send.at[face], recv.at[there], neighbours[face]
            )
            copy.start()
            copies[there] = copy
        return copies

    def difference(mine, theirs, face):
        value = mine - theirs
        return value if paired[face] is None else jnp.where(paired[face], value, 0.0)

    fetches = [
        pltpu.make_async_copy(source.at[0], dual, fetch_sem.at[0]),
        pltpu.make_async_copy(dirichlet.at[0], raw_dirichlet, fetch_sem.at[1]),
        pltpu.make_async_copy(neumann.at[0], raw_neumann, fetch_sem.at[2]),
    ]
    for fetch in fetches:
        fetch.start()
    barrier = pltpu.get_barrier_semaphore()

    def greet_group(step, carry):
        pl.semaphore_signal(barrier, inc=1, device_id=in_group(step)[1], device_id_type=MESH)
        return carry

    def greet_z(step, carry):
        pl.semaphore_signal(barrier, inc=1, device_id=along_z(step), device_id_type=MESH)
        return carry

    pl.semaphore_signal(barrier, inc=1, device_id=left, device_id_type=MESH)
    pl.semaphore_signal(barrier, inc=1, device_id=right, device_id_type=MESH)
    lax.fori_loop(1, GROUP, greet_group, 0)
    lax.fori_loop(1, NZ, greet_z, 0)

    lanes = lax.broadcasted_iota(jnp.int32, (1, 64), 1)
    down = lax.broadcasted_iota(jnp.int32, (256, 256), 0)
    for i in range(2):
        target = jnp.concatenate([lanes, face_map[0, i : i + 1, :] + 64], axis=1)
        perms[i] = (jnp.broadcast_to(target, (256, 256)) == down).astype(F32).astype(BF16)
    windows = (pl.ds(128, 256), pl.ds(512, 256))

    across = lax.broadcasted_iota(jnp.int32, (128, M), 0)
    scattered = jnp.zeros((128, M), F32)
    for j in range(4):
        scattered += jnp.where(across == corner_map[0, j] - BASE * z + NX, coupling[0, j : j + 1, :], 0.0)
    frame[...] = scattered.T
    for i in range(2):
        frame[windows[i], :] = permuted(perms[i], frame[windows[i], :])
    for face in range(4):
        value = frame[rows(face), :]
        if face == 0:
            value = jnp.where(place == 0, pltpu.roll(value, BASE, 1), value)
        if face == 1:
            value = jnp.where(place == PLANE - 1, pltpu.roll(value, 128 - BASE, 1), value)
        corner_out[face] = value[: FACE // 2] + pltpu.roll(value[FACE // 2 :], 64, 1)

    fetches[0].wait()
    for i in range(2):
        dual[windows[i], :] = permuted(perms[i], dual[windows[i], :])

    pl.semaphore_wait(barrier, GROUP - 1 + NZ - 1 + 2)

    faces = send_faces(dual, local_in, face_send, source_recv)
    corners = [None] * 4
    for face in range(4):
        there = partner_face[face]
        copy = remote(
            corner_out.at[face], corner_in.at[there], corner_send.at[face], corner_recv.at[there], neighbours[face]
        )
        copy.start()
        corners[there] = copy

    blocks[coarse, 0:129, :] = coarse_inverse[...]
    blocks[coarse, 129:144, :] = jnp.zeros((15, 516), F32)
    assembled[...] = jnp.zeros((WIDE, WIDE), F32)
    solved[...] = jnp.zeros((M, K), F32)
    search[...] = jnp.zeros((M, K), F32)
    image[...] = jnp.zeros((M, K), F32)
    scalars[...] = jnp.ones((8, K), F32)
    shifted[...] = jnp.zeros((7, 8, 128), F32)

    def reorder(raw, out, first):
        for i in range(2):
            raw[windows[i], :] = dot(perms[i], raw[windows[i], :]).astype(BF16)
        out[pl.ds(first, M), 0:128] = raw[:, 0:128]
        out[pl.ds(first, M), 384:512] = raw[:, 384:512]
        for i in range(2):
            out[pl.ds(first, M), windows[i]] = dot_nt(raw[:, windows[i]], perms[i]).astype(BF16)

    fetches[1].wait()
    reorder(raw_dirichlet, dirichlet_all, 128)
    fetches[2].wait()
    reorder(raw_neumann, neumann_own, 0)

    for face in range(4):
        faces[face].wait_recv()
        residual[rows(face), :] = difference(dual[rows(face), :], local_in[rows(face), :], face)

    low_lane = lax.broadcasted_iota(jnp.int32, (FACE // 2, 128), 1) < 64
    for face in range(4):
        corners[face].wait_recv()
        packed = corner_in[face]
        theirs = jnp.concatenate(
            [jnp.where(low_lane, packed, 0.0), jnp.where(low_lane, pltpu.roll(packed, 64, 1), 0.0)], axis=0
        )
        frame[rows(face), :] = difference(frame[rows(face), :], theirs, face)
    jumped = frame[...]
    high = rounded(jumped)
    low = jumped - high
    spread[...] = jnp.concatenate([high + pltpu.roll(low, 64, 1), high], axis=1).astype(BF16)
    jumped_t = jumped.T[0:64]
    high_t = rounded(jumped_t)
    product = dot(
        jnp.concatenate([high_t, jumped_t - high_t], axis=0).astype(BF16), dirichlet_all[pl.ds(128, M), :]
    )
    product = product[0:64] + product[64:128]
    high_t = rounded(product)
    dirichlet_all[0:128, :] = jnp.concatenate([high_t, product - high_t], axis=0).astype(BF16)
    for face in range(4):
        faces[face].wait_send()
        corners[face].wait_send()

    lane = lax.broadcasted_iota(jnp.int32, (8, 128), 1)

    def iteration(k, carry):
        scaled = (0.5 * residual[...]).astype(BF16)
        weighted[...] = dot(dirichlet_all[pl.ds(128, M), :], scaled)
        weighted_copies = send_faces(weighted, weighted_in, face_send, weighted_recv)
        load = dot(dirichlet_all[0:128, :], scaled)
        load = 0.5 * (load[0:64] + load[64:128])
        load = jnp.concatenate([load, jnp.zeros((64, K), F32)], axis=0)
        loads_out[...] = load.T.reshape(GROUP, 8, 128)
        loads_in[own] = loads_out[own]

        def send_load(step, carry):
            peer, device = in_group(step)
            remote(loads_out.at[peer], loads_in.at[own], group_send, loads_recv, device).start()
            return carry

        lax.fori_loop(1, GROUP, send_load, 0)

        @pl.when(k == 0)
        def _():
            half = pl.ds(pl.multiple_of(core * 72, 8), 72)
            for step in range(1, NX):
                device = (region, lax.rem(coarse + step, NX))
                remote(
                    blocks.at[coarse, half], blocks.at[coarse, half], block_send.at[step], block_recv.at[step], device
                ).start()

        u = weighted[...]
        first_sum = jnp.sum(residual[...] * u, axis=0, keepdims=True)
        second_sum = jnp.sum(image[...] * u, axis=0, keepdims=True)

        drain(loads_in.at[pl.ds(0, GROUP - 1)], loads_recv)
        plane_loads[...] = jnp.sum(loads_in[...], axis=0)
        all_loads[k, z] = plane_loads[...]

        def send_plane(i, carry):
            step = 8 + jnp.where(lax.rem(i, 2) == 1, -lax.div(i + 1, 2), lax.div(i, 2))
            remote(plane_loads, all_loads.at[k, z], plane_send, all_recv.at[k], along_z(step)).start()
            return carry

        lax.fori_loop(0, NZ - 1, send_plane, 0)

        for face in range(4):
            weighted_copies[face].wait_recv()
            dual[rows(face), :] = 0.5 * difference(weighted[rows(face), :], weighted_in[rows(face), :], face)
        local[...] = dot(neumann_own[...], dual[...].astype(BF16))
        for face in range(4):
            weighted_copies[face].wait_send()
        local_copies = send_faces(local, local_in, face_send, local_recv)
        third_sum = jnp.sum(dual[...] * local[...], axis=0, keepdims=True)
        dots_out[...] = jnp.concatenate(
            [v[:, h : h + 128] for v in (third_sum, first_sum, second_sum) for h in (0, 128)]
            + [jnp.zeros((2, 128), F32)],
            axis=0,
        )
        all_dots[k, z] = dots_out[...]

        def send_dots(i, carry):
            step = 8 + jnp.where(lax.rem(i, 2) == 1, -lax.div(i + 1, 2), lax.div(i, 2))
            remote(dots_out, all_dots.at[k, z], dots_send, dots_recv.at[k], along_z(step)).start()
            return carry

        lax.fori_loop(0, NZ - 1, send_dots, 0)

        @pl.when(k == 0)
        def _():
            half = pl.ds(pl.multiple_of(core * 72, 8), 72)
            other = (region + 1 - 2 * core, coarse)
            here = [lax.rem(coarse + NX - step, NX) for step in range(1, NX)]
            copies = [
                remote(blocks.at[i, half], blocks.at[i, half], core_send.at[s], core_recv.at[s], other)
                for s, i in enumerate(here)
            ]
            for step in range(1, NX):
                remote(
                    blocks.at[coarse, half],
                    blocks.at[here[step - 1], half],
                    block_send.at[step],
                    block_recv.at[step],
                    other,
                ).wait_recv()
                copies[step - 1].start()
            for copy in copies:
                copy.wait()
            for step in range(1, NX):
                drain(blocks.at[coarse, half], block_send.at[step])
            for i in range(NX):
                assembled[129 * i : 129 * (i + 1), 0:516] = blocks[i, 0:129, :]
            whole = assembled[...]
            inverse_high[...] = whole.astype(BF16)
            inverse_low[...] = (whole - rounded(whole)).astype(BF16)

        drain(all_loads.at[k, pl.ds(0, NZ - 1)], all_recv.at[k])
        part = [all_loads[k, i] for i in range(NZ)]
        tiles = []
        for t in range(5):
            tile = jnp.zeros((8, 128), F32)
            if t < 4:
                tile += jnp.where(lane < 124, pltpu.roll(part[4 * t], 124, 1), 0.0)
                tile += pltpu.roll(part[4 * t + 1], 28, 1) + pltpu.roll(part[4 * t + 2], 60, 1)
                tile += jnp.where(lane >= 64, pltpu.roll(part[4 * t + 3], 92, 1), 0.0)
            if t < 3:
                tile += jnp.where(lane >= 124, pltpu.roll(part[4 * t + 4], 124, 1), 0.0)
            if t > 0:
                tile += jnp.where(lane < 64, pltpu.roll(part[4 * t - 1], 92, 1), 0.0)
            tiles.append(tile)
        totals = jnp.concatenate(tiles, axis=1)
        high = rounded(totals)
        both = jnp.concatenate([high, totals - high], axis=0).astype(BF16)
        values = dot(both, inverse_high[...]) + dot(both, inverse_low[...])
        values = values[0:8] + values[8:16]
        energy = jnp.sum(totals * values, axis=1, keepdims=True)
        for t in range(5):
            shifted[t + 1] = values[:, 128 * t : 128 * (t + 1)]
        quarter, turn = lax.div(z, 4), lax.rem(z, 4)
        now, nearby, later = shifted[quarter], shifted[quarter + 1], shifted[quarter + 2]
        framed = jnp.where(
            turn == 0,
            jnp.where(lane < 4, pltpu.roll(now, 4, 1), pltpu.roll(nearby, 4, 1)),
            jnp.where(
                turn == 1,
                pltpu.roll(nearby, 100, 1),
                jnp.where(
                    turn == 2,
                    pltpu.roll(nearby, 68, 1),
                    jnp.where(lane < 36, pltpu.roll(nearby, 36, 1), pltpu.roll(later, 36, 1)),
                ),
            ),
        )
        framed = jnp.where(lane < USED, framed, jnp.where(lane == USED, energy, 0.0))

        drain(all_dots.at[k, pl.ds(0, NZ - 1)], dots_recv.at[k])
        back_out[0:8] = framed
        back_out[8:16] = jnp.sum(all_dots[k], axis=0)
        back_in[own] = back_out[...]

        def send_back(step, carry):
            device = in_group(step)[1]
            remote(back_out, back_in.at[own], back_send, back_recv, device).start()
            return carry

        lax.fori_loop(1, GROUP, send_back, 0)

        for face in range(4):
            local_copies[face].wait_recv()
        drain(back_in.at[pl.ds(0, GROUP - 1)], back_recv)
        coarse_values = back_in[:, 0:8, :].reshape(K, 128).T
        sums = jnp.sum(back_in[:, 8:16, :], axis=0)

        def joined(i):
            return jnp.concatenate([sums[i : i + 1], sums[i + 1 : i + 2]], axis=1)

        curve = 2.0 * (joined(0) + coarse_values[USED : USED + 1])
        product_sum = joined(2)
        ratio = jnp.where(k > 0, product_sum / scalars[0:1], 0.0)
        curve = curve + 2.0 * ratio * joined(4)
        curve = curve + jnp.where(k > 0, ratio * ratio * scalars[1:2], 0.0)
        step_len = product_sum / curve
        scalars[0:1] = product_sum
        scalars[1:2] = curve
        values_high = rounded(coarse_values[0:64])
        stacked = jnp.concatenate(
            [values_high, values_high, coarse_values[0:64] - values_high, jnp.zeros((64, K), F32)], axis=0
        ).astype(BF16)
        for face in range(4):
            at = rows(face)
            own_image = difference(local[at, :], local_in[at, :], face) + dot(spread[at, :], stacked)
            new_image = own_image + ratio * image[at, :]
            new_search = dual[at, :] + ratio * search[at, :]
            image[at, :] = new_image
            search[at, :] = new_search
            solved[at, :] += step_len * new_search
            residual[at, :] -= step_len * new_image

        for face in range(4):
            local_copies[face].wait_send()
        drain(loads_out.at[pl.ds(0, GROUP - 1)], group_send)
        drain(all_loads.at[k, pl.ds(0, NZ - 1)], plane_send)
        drain(all_dots.at[k, pl.ds(0, NZ - 1)], dots_send)
        drain(back_in.at[pl.ds(0, GROUP - 1)], back_send)
        return carry

    lax.fori_loop(0, ITERS, iteration, 0)

    for value, out in ((solved, x_out), (residual, r_out)):
        out[0, 0:128, :] = value[0:128, :]
        out[0, 384:512, :] = value[384:512, :]
        for i in range(2):
            out[0, windows[i], :] = permuted(perms[i].astype(F32).T.astype(BF16), value[windows[i], :])


def body(source, neumann, dirichlet, coupling, corner_map, face_map, coarse_inverse):
    field = pltpu.VMEM((M, K), F32)
    square = pltpu.VMEM((M, M), BF16)
    dma, one = pltpu.SemaphoreType.DMA, pltpu.SemaphoreType.DMA(())
    scratch = [
        field, field, field, field, field, field, field,
        field, field,
        pltpu.VMEM((4, FACE // 2, 128), F32), pltpu.VMEM((4, FACE // 2, 128), F32), pltpu.VMEM((M, 128), F32),
        pltpu.VMEM((2, 256, 256), BF16), pltpu.VMEM((M + 128, M), BF16), square, square, square,
        pltpu.VMEM((M, 256), BF16),
        pltpu.VMEM((NX, 144, 516), F32), pltpu.VMEM((WIDE, WIDE), F32),
        pltpu.VMEM((WIDE, WIDE), BF16), pltpu.VMEM((WIDE, WIDE), BF16),
        pltpu.VMEM((7, 8, 128), F32), pltpu.VMEM((8, K), F32),
        pltpu.VMEM((GROUP, 8, 128), F32), pltpu.VMEM((GROUP, 8, 128), F32),
        pltpu.VMEM((8, 128), F32), pltpu.VMEM((ITERS, NZ, 8, 128), F32),
        pltpu.VMEM((8, 128), F32), pltpu.VMEM((ITERS, NZ, 8, 128), F32),
        pltpu.VMEM((16, 128), F32), pltpu.VMEM((GROUP, 16, 128), F32),
        dma((3,)), dma((4,)), dma((4,)), dma((4,)), dma((4,)), dma((4,)), dma((4,)),
        dma((4,)), dma((4,)), dma((3,)), dma((3,)),
        one, one, one, dma((ITERS,)), one, dma((ITERS,)), one, one,
    ]
    vmem, hbm = pl.BlockSpec(memory_space=pltpu.VMEM), pl.BlockSpec(memory_space=pl.ANY)
    return pl.pallas_call(
        kernel,
        out_shape=(jax.ShapeDtypeStruct((1, M, K), F32), jax.ShapeDtypeStruct((1, M, K), F32)),
        in_specs=[hbm, hbm, hbm, vmem, pl.BlockSpec(memory_space=pltpu.SMEM), vmem, vmem],
        out_specs=(vmem, vmem),
        scratch_shapes=scratch,
        compiler_params=pltpu.CompilerParams(collective_id=0, has_side_effects=True, vmem_limit_bytes=48 * 2**20),
        cost_estimate=pl.CostEstimate(flops=3 * 4 * M * M * K, bytes_accessed=6 * 10**6, transcendentals=0),
    )(source, neumann, dirichlet, coupling, corner_map, face_map, coarse_inverse)


def solution(mesh):
    split = P(("region", "coarse"), None, None)
    placed = (split, split, split, split, P(("region", "coarse"), None), split, P("coarse", None))
    return jax.shard_map(body, mesh=mesh, in_specs=placed, out_specs=(split, split), check_vma=False)
```

time: 2190 us -> 125 us (0.06)
  waiting for transfers between devices: 1420 us -> 0 us
  blocking collectives: 550 us -> 0 us
  Pallas kernels: 0 us -> 116 us
  starting transfers between devices: 97.5 us -> 0 us
  other arithmetic: 42.1 us -> 0 us
  local copies, waits for them, and re-layouts: 40.7 us -> 8.45 us
  matrix products: 23 us -> 0 us
    psum x3 -> x0, waiting for transfers between devices: 1360 us -> none  [coarse_solve(): totals = lax.psum(scattered, ('region', 'coarse'))]
    psum x5 -> x0, blocking collectives: 516 us -> none  [the longest x3 310 us: precond_apply(): return (precond, lax.psum(local_sum, ('region', 'coarse')))]
    pallas_call x0 -> x1, Pallas kernels: none -> 116 us  [body(): pl.pallas_call(kernel, out_shape=(jax.ShapeDtypeStruct((1, M, K), F32), j...]
    ppermute x28 -> x0, starting transfers between devices: 97.4 us -> none  [the longest x14 55.9 us: extended(): after = lax.ppermute(initial, axis, down)]
    ppermute x28 -> x0, waiting for transfers between devices: 55.8 us -> none  [the longest x14 29 us: extended(): after = lax.ppermute(initial, axis, down)]
    all_gather x3 -> x0, blocking collectives: 34 us -> none  [coarse_solve(): return lax.all_gather(owned, 'coarse', axis=0, tiled=True)]
    gather x28 -> x0, local copies, waits for them, and re-layouts: 33 us -> none  [the longest x7 8.36 us: dual_jump(): jnp.take(faces[1], backward[0], axis=0)]
    dot_general x21 -> x0, matrix products: 23 us -> none  [the longest x3 5.71 us: neumann_apply(): jnp.dot(neumann_inverse[0], direction[0].astype(jnp.bfloat16), preferred_...]
  transfers between devices with their start and end apart: 31 -> 0, of which waited for: 23 -> 0; matrix products, arithmetic and copies ran while one was open for 1% -> 0% of each run, Pallas kernels for 0% -> 0%
where the time goes in v1:
time: 125 us
  Pallas kernels  116 us (93%)
  local copies, waits for them, and re-layouts  8.45 us (7%)
    pallas_call x1, Pallas kernels, body(): pl.pallas_call(kernel, out_shape=(jax.ShapeDtypeStruct((1, M, K), F32), j...  116 us
    unnamed x16, local copies, waits for them, and re-layouts  8.45 us

profile of v1, /device:TPU:1, one launch (start us, length us, event | category | flops | bytes accessed | tf_op | source)
XLA Modules:
  0.0 124.8 jit_solution(7908306300750359985)
XLA Ops:
  0.6 0.0 copy-start
  0.6 1.3 %copy-done = bf16[1,768,768]{2,1,0:T(8,128)(2,1)S(1)} copy-done((bf16[1,768,768]{2,1,0:T(8,128)(2,1)S(1)}, bf16[1,768,768]{2,1,0:T(8,128)(2,1)}, u32[]{:S(2)}) %copy-start) | copy-done | bytes 1179672
  1.9 0.0 copy-start.1
  1.9 1.3 %copy-done.1 = bf16[1,768,768]{2,1,0:T(8,128)(2,1)S(1)} copy-done((bf16[1,768,768]{2,1,0:T(8,128)(2,1)S(1)}, bf16[1,768,768]{2,1,0:T(8,128)(2,1)}, u32[]{:S(2)}) %copy-start.1) | copy-done | bytes 1179672
  3.2 0.0 copy-start.2
  3.2 1.1 copy-done.2
  4.3 0.0 copy-start.3
  4.3 1.0 copy-done.3
  5.3 0.0 copy-start.4
  5.3 0.7 copy-done.4
  6.0 0.0 copy-start.5
  6.0 0.7 copy-done.5
  6.7 0.0 copy-start.6
  6.7 0.7 copy-done.6
  7.3 115.7 %shard_map.86 = (f32[1,768,256]{2,1,0:T(8,128)S(1)}, f32[1,768,256]{2,1,0:T(8,128)S(1)}) custom-call(f32[1,768,256]{2,1,0:T(8,128)S(1)} %copy-done.2, bf16[1,768,768]{2,1,0:T(8,128)(2,1)S(1)} %copy-done, bf16[1,768,768]{2,1,0:T(8,128)(2,1)S(1)} %copy-done.1, f32[1,4,768]{2,1,0:T(4,128)S(1)} %copy-done.4, s32[1,4]{1,0:T(1,128)S(1)} %copy-done.6, ...), custom_call_target="tpu_custom_call" | custom-call | flops 1811939328 | bytes 6000000 | tf_op jit(solution)/shard_map/pallas_call | solution.py:428
  123.0 0.9 copy.11
  123.9 0.9 copy.12
Async XLA Ops:
  0.6 1.3 %copy-start = (bf16[1,768,768]{2,1,0:T(8,128)(2,1)S(1)}, bf16[1,768,768]{2,1,0:T(8,128)(2,1)}, u32[]{:S(2)}) copy-start(bf16[1,768,768]{2,1,0:T(8,128)(2,1)} %neumann.1) | copy-start | bytes 3538948
  1.9 1.3 %copy-start.1 = (bf16[1,768,768]{2,1,0:T(8,128)(2,1)S(1)}, bf16[1,768,768]{2,1,0:T(8,128)(2,1)}, u32[]{:S(2)}) copy-start(bf16[1,768,768]{2,1,0:T(8,128)(2,1)} %dirichlet.1) | copy-start | bytes 3538948
  3.2 1.1 copy-start.2
  4.3 1.0 copy-start.3
  5.3 0.7 copy-start.4
  6.0 0.7 copy-start.5
  6.7 0.7 copy-start.6

commit v2 on v1

--- a/solution.py
+++ b/solution.py
@@ -21,6 +21,17 @@
 BASE = NX * PLANE
 USED = NX * (PLANE + 3)
 WIDE = 640
+
+
+def hops(step):
+    return min(step, 4 - step)
+
+
+MEMBERS = sorted(
+    ((dy, dx, dc) for dy in range(4) for dx in range(4) for dc in range(2) if (dy, dx, dc) != (0, 0, 0)),
+    key=lambda d: (-hops(d[0]) - hops(d[1]), d),
+)
+PLANES = sorted(range(1, NZ), key=lambda step: -min(step, NZ - step))
 
 
 def rounded(value):
@@ -68,12 +79,13 @@
     partner_face = (1, 0, 3, 2)
     paired = (region > 0, region < n_region - 1, None, None)
 
-    def in_group(step):
-        peer = lax.rem(own + step, GROUP)
-        return peer, (z * PLANE + lax.div(peer, NX), lax.rem(peer, NX))
-
-    def along_z(step):
-        return (lax.rem(z + step, NZ) * PLANE + place, coarse)
+    row = lax.div(place, 2)
+    members = []
+    for dy, dx, dc in MEMBERS:
+        there = 2 * lax.rem(row + dy, 4) + (1 - core if dc else core)
+        x = lax.rem(coarse + dx, NX)
+        members.append((there * NX + x, (z * PLANE + there, x)))
+    planes = [(lax.rem(z + step, NZ) * PLANE + place, coarse) for step in PLANES]
 
     def rows(face):
         return pl.ds(face * FACE, FACE)
@@ -110,18 +122,8 @@
         fetch.start()
     barrier = pltpu.get_barrier_semaphore()
 
-    def greet_group(step, carry):
-        pl.semaphore_signal(barrier, inc=1, device_id=in_group(step)[1], device_id_type=MESH)
-        return carry
-
-    def greet_z(step, carry):
-        pl.semaphore_signal(barrier, inc=1, device_id=along_z(step), device_id_type=MESH)
-        return carry
-
-    pl.semaphore_signal(barrier, inc=1, device_id=left, device_id_type=MESH)
-    pl.semaphore_signal(barrier, inc=1, device_id=right, device_id_type=MESH)
-    lax.fori_loop(1, GROUP, greet_group, 0)
-    lax.fori_loop(1, NZ, greet_z, 0)
+    for device in planes + [device for _, device in members] + [left, right]:
+        pl.semaphore_signal(barrier, inc=1, device_id=device, device_id_type=MESH)
 
     lanes = lax.broadcasted_iota(jnp.int32, (1, 64), 1)
     down = lax.broadcasted_iota(jnp.int32, (256, 256), 0)
@@ -151,7 +153,6 @@
 
     pl.semaphore_wait(barrier, GROUP - 1 + NZ - 1 + 2)
 
-    faces = send_faces(dual, local_in, face_send, source_recv)
     corners = [None] * 4
     for face in range(4):
         there = partner_face[face]
@@ -160,9 +161,16 @@
         )
         copy.start()
         corners[there] = copy
+    faces = send_faces(dual, local_in, face_send, source_recv)
+    half = pl.ds(pl.multiple_of(core * 72, 8), 72)
+
+    def block_copy(i, sem, device):
+        return remote(blocks.at[i, half], blocks.at[i, half], block_send.at[sem], block_recv.at[sem], device)
 
     blocks[coarse, 0:129, :] = coarse_inverse[...]
     blocks[coarse, 129:144, :] = jnp.zeros((15, 516), F32)
+    block_copy(coarse, 0, after).start()
+    block_copy(coarse, 1, before).start()
     assembled[...] = jnp.zeros((WIDE, WIDE), F32)
     solved[...] = jnp.zeros((M, K), F32)
     search[...] = jnp.zeros((M, K), F32)
@@ -182,10 +190,6 @@
     reorder(raw_dirichlet, dirichlet_all, 128)
     fetches[2].wait()
     reorder(raw_neumann, neumann_own, 0)
-
-    for face in range(4):
-        faces[face].wait_recv()
-        residual[rows(face), :] = difference(dual[rows(face), :], local_in[rows(face), :], face)
 
     low_lane = lax.broadcasted_iota(jnp.int32, (FACE // 2, 128), 1) < 64
     for face in range(4):
@@ -208,36 +212,44 @@
     high_t = rounded(product)
     dirichlet_all[0:128, :] = jnp.concatenate([high_t, product - high_t], axis=0).astype(BF16)
     for face in range(4):
+        faces[face].wait_recv()
+        residual[rows(face), :] = difference(dual[rows(face), :], local_in[rows(face), :], face)
+    for face in range(4):
         faces[face].wait_send()
         corners[face].wait_send()
 
     lane = lax.broadcasted_iota(jnp.int32, (8, 128), 1)
 
+    def update():
+        for face in range(4):
+            at = rows(face)
+            new_search = dual[at, :] + scalars[2:3] * search[at, :]
+            search[at, :] = new_search
+            solved[at, :] += scalars[3:4] * new_search
+
     def iteration(k, carry):
         scaled = (0.5 * residual[...]).astype(BF16)
-        weighted[...] = dot(dirichlet_all[pl.ds(128, M), :], scaled)
-        weighted_copies = send_faces(weighted, weighted_in, face_send, weighted_recv)
         load = dot(dirichlet_all[0:128, :], scaled)
         load = 0.5 * (load[0:64] + load[64:128])
         load = jnp.concatenate([load, jnp.zeros((64, K), F32)], axis=0)
         loads_out[...] = load.T.reshape(GROUP, 8, 128)
         loads_in[own] = loads_out[own]
 
-        def send_load(step, carry):
-            peer, device = in_group(step)
+        for peer, device in members:
             remote(loads_out.at[peer], loads_in.at[own], group_send, loads_recv, device).start()
-            return carry
-
-        lax.fori_loop(1, GROUP, send_load, 0)
+        weighted[...] = dot(dirichlet_all[pl.ds(128, M), :], scaled)
+        weighted_copies = send_faces(weighted, weighted_in, face_send, weighted_recv)
+
+        @pl.when(k > 0)
+        def _():
+            update()
 
         @pl.when(k == 0)
         def _():
-            half = pl.ds(pl.multiple_of(core * 72, 8), 72)
-            for step in range(1, NX):
-                device = (region, lax.rem(coarse + step, NX))
-                remote(
-                    blocks.at[coarse, half], blocks.at[coarse, half], block_send.at[step], block_recv.at[step], device
-                ).start()
+            for sem in range(2):
+                block_copy(coarse, sem, after).wait()
+            turn = 1 - 2 * core
+            block_copy(lax.rem(coarse + NX - turn, NX), 2, (region, lax.rem(coarse + NX + turn, NX))).start()
 
         u = weighted[...]
         first_sum = jnp.sum(residual[...] * u, axis=0, keepdims=True)
@@ -247,12 +259,8 @@
         plane_loads[...] = jnp.sum(loads_in[...], axis=0)
         all_loads[k, z] = plane_loads[...]
 
-        def send_plane(i, carry):
-            step = 8 + jnp.where(lax.rem(i, 2) == 1, -lax.div(i + 1, 2), lax.div(i, 2))
-            remote(plane_loads, all_loads.at[k, z], plane_send, all_recv.at[k], along_z(step)).start()
-            return carry
-
-        lax.fori_loop(0, NZ - 1, send_plane, 0)
+        for device in planes:
+            remote(plane_loads, all_loads.at[k, z], plane_send, all_recv.at[k], device).start()
 
         for face in range(4):
             weighted_copies[face].wait_recv()
@@ -260,7 +268,6 @@
         local[...] = dot(neumann_own[...], dual[...].astype(BF16))
         for face in range(4):
             weighted_copies[face].wait_send()
-        local_copies = send_faces(local, local_in, face_send, local_recv)
         third_sum = jnp.sum(dual[...] * local[...], axis=0, keepdims=True)
         dots_out[...] = jnp.concatenate(
             [v[:, h : h + 128] for v in (third_sum, first_sum, second_sum) for h in (0, 128)]
@@ -269,35 +276,25 @@
         )
         all_dots[k, z] = dots_out[...]
 
-        def send_dots(i, carry):
-            step = 8 + jnp.where(lax.rem(i, 2) == 1, -lax.div(i + 1, 2), lax.div(i, 2))
-            remote(dots_out, all_dots.at[k, z], dots_send, dots_recv.at[k], along_z(step)).start()
-            return carry
-
-        lax.fori_loop(0, NZ - 1, send_dots, 0)
+        for device in planes:
+            remote(dots_out, all_dots.at[k, z], dots_send, dots_recv.at[k], device).start()
+        local_copies = send_faces(local, local_in, face_send, local_recv)
 
         @pl.when(k == 0)
         def _():
-            half = pl.ds(pl.multiple_of(core * 72, 8), 72)
+            block_copy(coarse, 2, after).wait()
             other = (region + 1 - 2 * core, coarse)
-            here = [lax.rem(coarse + NX - step, NX) for step in range(1, NX)]
-            copies = [
-                remote(blocks.at[i, half], blocks.at[i, half], core_send.at[s], core_recv.at[s], other)
-                for s, i in enumerate(here)
-            ]
+            copies = []
             for step in range(1, NX):
-                remote(
-                    blocks.at[coarse, half],
-                    blocks.at[here[step - 1], half],
-                    block_send.at[step],
-                    block_recv.at[step],
-                    other,
-                ).wait_recv()
-                copies[step - 1].start()
+                i = lax.rem(coarse + step, NX)
+                copies.append(
+                    remote(
+                        blocks.at[i, half], blocks.at[i, half], core_send.at[step - 1], core_recv.at[step - 1], other
+                    )
+                )
+                copies[-1].start()
             for copy in copies:
                 copy.wait()
-            for step in range(1, NX):
-                drain(blocks.at[coarse, half], block_send.at[step])
             for i in range(NX):
                 assembled[129 * i : 129 * (i + 1), 0:516] = blocks[i, 0:129, :]
             whole = assembled[...]
@@ -348,15 +345,14 @@
         back_out[8:16] = jnp.sum(all_dots[k], axis=0)
         back_in[own] = back_out[...]
 
-        def send_back(step, carry):
-            device = in_group(step)[1]
+        for _, device in members:
             remote(back_out, back_in.at[own], back_send, back_recv, device).start()
-            return carry
-
-        lax.fori_loop(1, GROUP, send_back, 0)
-
+
+        for face in range(4):
+            local_copies[face].wait_send()
         for face in range(4):
             local_copies[face].wait_recv()
+            local[rows(face), :] = difference(local[rows(face), :], local_in[rows(face), :], face)
         drain(back_in.at[pl.ds(0, GROUP - 1)], back_recv)
         coarse_values = back_in[:, 0:8, :].reshape(K, 128).T
         sums = jnp.sum(back_in[:, 8:16, :], axis=0)
@@ -376,18 +372,14 @@
         stacked = jnp.concatenate(
             [values_high, values_high, coarse_values[0:64] - values_high, jnp.zeros((64, K), F32)], axis=0
         ).astype(BF16)
+        scalars[2:3] = ratio
+        scalars[3:4] = step_len
         for face in range(4):
             at = rows(face)
-            own_image = difference(local[at, :], local_in[at, :], face) + dot(spread[at, :], stacked)
-            new_image = own_image + ratio * image[at, :]
-            new_search = dual[at, :] + ratio * search[at, :]
+            new_image = local[at, :] + dot(spread[at, :], stacked) + ratio * image[at, :]
             image[at, :] = new_image
-            search[at, :] = new_search
-            solved[at, :] += step_len * new_search
             residual[at, :] -= step_len * new_image
 
-        for face in range(4):
-            local_copies[face].wait_send()
         drain(loads_out.at[pl.ds(0, GROUP - 1)], group_send)
         drain(all_loads.at[k, pl.ds(0, NZ - 1)], plane_send)
         drain(all_dots.at[k, pl.ds(0, NZ - 1)], dots_send)
@@ -395,6 +387,7 @@
         return carry
 
     lax.fori_loop(0, ITERS, iteration, 0)
+    update()
 
     for value, out in ((solved, x_out), (residual, r_out)):
         out[0, 0:128, :] = value[0:128, :]
@@ -421,7 +414,7 @@
         pltpu.VMEM((8, 128), F32), pltpu.VMEM((ITERS, NZ, 8, 128), F32),
         pltpu.VMEM((16, 128), F32), pltpu.VMEM((GROUP, 16, 128), F32),
         dma((3,)), dma((4,)), dma((4,)), dma((4,)), dma((4,)), dma((4,)), dma((4,)),
-        dma((4,)), dma((4,)), dma((3,)), dma((3,)),
+        dma((3,)), dma((3,)), dma((3,)), dma((3,)),
         one, one, one, dma((ITERS,)), one, dma((ITERS,)), one, one,
     ]
     vmem, hbm = pl.BlockSpec(memory_space=pltpu.VMEM), pl.BlockSpec(memory_space=pl.ANY)
@@ -431,7 +424,7 @@
         in_specs=[hbm, hbm, hbm, vmem, pl.BlockSpec(memory_space=pltpu.SMEM), vmem, vmem],
         out_specs=(vmem, vmem),
         scratch_shapes=scratch,
-        compiler_params=pltpu.CompilerParams(collective_id=0, has_side_effects=True, vmem_limit_bytes=48 * 2**20),
+        compiler_params=pltpu.CompilerParams(collective_id=0, has_side_effects=True, vmem_limit_bytes=62 * 2**20),
         cost_estimate=pl.CostEstimate(flops=3 * 4 * M * M * K, bytes_accessed=6 * 10**6, transcendentals=0),
     )(source, neumann, dirichlet, coupling, corner_map, face_map, coarse_inverse)
 

time: 125 us -> 99.2 us (0.79)
  Pallas kernels: 116 us -> 95.3 us
  local copies, waits for them, and re-layouts: 8.45 us -> 3.02 us
    pallas_call x1, Pallas kernels: 116 us -> 95.3 us  [body(): pl.pallas_call(kernel, out_shape=(jax.ShapeDtypeStruct((1, M, K), F32), j...]
    unnamed x16 -> x4, local copies, waits for them, and re-layouts: 8.45 us -> 3.02 us
where the time goes in v2:
time: 99.2 us; the launch traced here: 99 us
  Pallas kernels  95.3 us (96%)
  local copies, waits for them, and re-layouts  3.02 us (3%)
    pallas_call x1, Pallas kernels, body(): pl.pallas_call(kernel, out_shape=(jax.ShapeDtypeStruct((1, M, K), F32), j...  95.3 us
    unnamed x4, local copies, waits for them, and re-layouts  3.02 us

profile of v2, /device:TPU:1, one launch (start us, length us, event | category | flops | bytes accessed | tf_op | source)
XLA Modules:
  0.0 99.0 jit_solution(15066574818459059764)
XLA Ops:
  0.6 95.3 %shard_map.86 = (f32[1,768,256]{2,1,0:T(8,128)}, f32[1,768,256]{2,1,0:T(8,128)}) custom-call(f32[1,768,256]{2,1,0:T(8,128)} %source.1, bf16[1,768,768]{2,1,0:T(8,128)(2,1)} %neumann.1, bf16[1,768,768]{2,1,0:T(8,128)(2,1)} %dirichlet.1, f32[1,4,768]{2,1,0:T(4,128)} %coupling.1, s32[1,4]{1,0:T(1,128)} %corner_map.1, s32[1,2,192]{2,1,0:T(2,128)} %face_map.1, ...), custom_call_target="tpu_custom_call" | custom-call | flops 1811939328 | bytes 6000000 | tf_op jit(solution)/shard_map/pallas_call | solution.py:421
  96.0 0.0 copy-start
  96.0 2.1 %copy.11 = f32[1,768,256]{2,1,0:T(8,128)} copy(f32[1,768,256]{2,1,0:T(8,128)} %get-tuple-element.4) | data formatting | bytes 1572864
  98.1 0.0 copy-done
  98.1 0.9 copy.12
Async XLA Ops:
  96.0 2.1 %copy-start = (f32[1,768,256]{2,1,0:T(8,128)S(1)}, f32[1,768,256]{2,1,0:T(8,128)}, u32[]{:S(2)}) copy-start(f32[1,768,256]{2,1,0:T(8,128)} %get-tuple-element.5) | copy-start | bytes 2359300

commit v3 on v2

--- a/solution.py
+++ b/solution.py
@@ -54,15 +54,26 @@
     return (dot(onehot, high) + dot(onehot, middle)) + dot(onehot, low)
 
 
+WINDOWS = (pl.ds(128, 256), pl.ds(512, 256))
+
+
+def one_hots(face_map, out):
+    lanes = lax.broadcasted_iota(jnp.int32, (1, 64), 1)
+    down = lax.broadcasted_iota(jnp.int32, (256, 256), 0)
+    for i in range(2):
+        target = jnp.concatenate([lanes, face_map[0, i : i + 1, :] + 64], axis=1)
+        out[i] = (jnp.broadcast_to(target, (256, 256)) == down).astype(F32).astype(BF16)
+
+
 def kernel(
-    source, neumann, dirichlet, coupling, corner_map, face_map, coarse_inverse,
-    x_out, r_out,
-    residual, solved, search, image, weighted, dual, local,
+    source, neumann, dirichlet, coupling_in, corner_map_in, face_map_in, coarse_inverse_in,
+    solved, residual,
+    coupling, corner_map, face_map, coarse_inverse, search, image, weighted, dual, local,
     weighted_in, local_in, corner_out, corner_in, frame,
     perms, dirichlet_all, neumann_own, raw_dirichlet, raw_neumann, spread,
     blocks, assembled, inverse_high, inverse_low, shifted, scalars,
     loads_out, loads_in, plane_loads, all_loads, dots_out, all_dots, back_out, back_in,
-    fetch_sem, face_send, source_recv, weighted_recv, local_recv, corner_send, corner_recv,
+    line_sem, near_sem, far_sem, fetch_sem, face_send, source_recv, weighted_recv, local_recv, corner_send, corner_recv,
     block_send, block_recv, core_send, core_recv,
     group_send, loads_recv, plane_send, all_recv, dots_send, dots_recv, back_send, back_recv,
 ):
@@ -100,7 +111,7 @@
 
     def send_faces(src, dst, send, recv):
         copies = [None] * 4
-        for face in range(4):
+        for face in (2, 3, 0, 1):
             there = partner_face[face]
             copy = remote(
                 src.at[rows(face)], dst.at[rows(there)], send.at[face], recv.at[there], neighbours[face]
@@ -113,32 +124,47 @@
         value = mine - theirs
         return value if paired[face] is None else jnp.where(paired[face], value, 0.0)
 
+    line = [(region, lax.rem(coarse + dx, NX)) for dx in range(1, NX)]
+    mates = [(z * PLANE + lax.rem(place + step, PLANE), coarse) for step in range(1, PLANE)]
+
+    def plane_at(step):
+        return (lax.rem(z + step + NZ, NZ) * PLANE + place, coarse)
+
+    def greet(sem, devices):
+        for device in devices:
+            pl.semaphore_signal(sem, inc=1, device_id=device, device_id_type=MESH)
+
+    barrier = pltpu.get_barrier_semaphore()
+    first_round = [plane_at(2), plane_at(-2), plane_at(1), plane_at(-1), left, right] + line + mates
+    greet(barrier, first_round)
     fetches = [
-        pltpu.make_async_copy(source.at[0], dual, fetch_sem.at[0]),
-        pltpu.make_async_copy(dirichlet.at[0], raw_dirichlet, fetch_sem.at[1]),
-        pltpu.make_async_copy(neumann.at[0], raw_neumann, fetch_sem.at[2]),
+        pltpu.make_async_copy(src, dst, fetch_sem.at[i])
+        for i, (src, dst) in enumerate(
+            (
+                (face_map_in, face_map),
+                (corner_map_in, corner_map),
+                (coupling_in, coupling),
+                (source.at[0], dual),
+                (dirichlet.at[0], raw_dirichlet),
+                (neumann.at[0], raw_neumann),
+                (coarse_inverse_in, coarse_inverse),
+            )
+        )
     ]
     for fetch in fetches:
         fetch.start()
-    barrier = pltpu.get_barrier_semaphore()
-
-    for device in planes + [device for _, device in members] + [left, right]:
-        pl.semaphore_signal(barrier, inc=1, device_id=device, device_id_type=MESH)
-
-    lanes = lax.broadcasted_iota(jnp.int32, (1, 64), 1)
-    down = lax.broadcasted_iota(jnp.int32, (256, 256), 0)
-    for i in range(2):
-        target = jnp.concatenate([lanes, face_map[0, i : i + 1, :] + 64], axis=1)
-        perms[i] = (jnp.broadcast_to(target, (256, 256)) == down).astype(F32).astype(BF16)
-    windows = (pl.ds(128, 256), pl.ds(512, 256))
+    for fetch in fetches[0:3]:
+        fetch.wait()
+
+    one_hots(face_map, perms)
 
     across = lax.broadcasted_iota(jnp.int32, (128, M), 0)
     scattered = jnp.zeros((128, M), F32)
     for j in range(4):
-        scattered += jnp.where(across == corner_map[0, j] - BASE * z + NX, coupling[0, j : j + 1, :], 0.0)
+        scattered += jnp.where(across == corner_map[0:1, j : j + 1] - BASE * z + NX, coupling[0, j : j + 1, :], 0.0)
     frame[...] = scattered.T
     for i in range(2):
-        frame[windows[i], :] = permuted(perms[i], frame[windows[i], :])
+        frame[WINDOWS[i], :] = permuted(perms[i], frame[WINDOWS[i], :])
     for face in range(4):
         value = frame[rows(face), :]
         if face == 0:
@@ -147,11 +173,11 @@
             value = jnp.where(place == PLANE - 1, pltpu.roll(value, 128 - BASE, 1), value)
         corner_out[face] = value[: FACE // 2] + pltpu.roll(value[FACE // 2 :], 64, 1)
 
-    fetches[0].wait()
+    fetches[3].wait()
     for i in range(2):
-        dual[windows[i], :] = permuted(perms[i], dual[windows[i], :])
-
-    pl.semaphore_wait(barrier, GROUP - 1 + NZ - 1 + 2)
+        dual[WINDOWS[i], :] = permuted(perms[i], dual[WINDOWS[i], :])
+
+    pl.semaphore_wait(barrier, len(first_round))
 
     corners = [None] * 4
     for face in range(4):
@@ -162,11 +188,14 @@
         copy.start()
         corners[there] = copy
     faces = send_faces(dual, local_in, face_send, source_recv)
+    greet(line_sem, line)
+    greet(near_sem, [plane_at(2), plane_at(-2)])
     half = pl.ds(pl.multiple_of(core * 72, 8), 72)
 
     def block_copy(i, sem, device):
         return remote(blocks.at[i, half], blocks.at[i, half], block_send.at[sem], block_recv.at[sem], device)
 
+    fetches[6].wait()
     blocks[coarse, 0:129, :] = coarse_inverse[...]
     blocks[coarse, 129:144, :] = jnp.zeros((15, 516), F32)
     block_copy(coarse, 0, after).start()
@@ -180,16 +209,18 @@
 
     def reorder(raw, out, first):
         for i in range(2):
-            raw[windows[i], :] = dot(perms[i], raw[windows[i], :]).astype(BF16)
+            raw[WINDOWS[i], :] = dot(perms[i], raw[WINDOWS[i], :]).astype(BF16)
         out[pl.ds(first, M), 0:128] = raw[:, 0:128]
         out[pl.ds(first, M), 384:512] = raw[:, 384:512]
         for i in range(2):
-            out[pl.ds(first, M), windows[i]] = dot_nt(raw[:, windows[i]], perms[i]).astype(BF16)
-
-    fetches[1].wait()
+            out[pl.ds(first, M), WINDOWS[i]] = dot_nt(raw[:, WINDOWS[i]], perms[i]).astype(BF16)
+
+    fetches[4].wait()
     reorder(raw_dirichlet, dirichlet_all, 128)
-    fetches[2].wait()
+    fetches[5].wait()
     reorder(raw_neumann, neumann_own, 0)
+    pl.semaphore_wait(near_sem, 2)
+    greet(far_sem, [plane_at(4), plane_at(-4)])
 
     low_lane = lax.broadcasted_iota(jnp.int32, (FACE // 2, 128), 1) < 64
     for face in range(4):
@@ -218,6 +249,7 @@
         faces[face].wait_send()
         corners[face].wait_send()
 
+    pl.semaphore_wait(line_sem, NX - 1)
     lane = lax.broadcasted_iota(jnp.int32, (8, 128), 1)
 
     def update():
@@ -255,6 +287,10 @@
         first_sum = jnp.sum(residual[...] * u, axis=0, keepdims=True)
         second_sum = jnp.sum(image[...] * u, axis=0, keepdims=True)
 
+        @pl.when(k == 0)
+        def _():
+            pl.semaphore_wait(far_sem, 2)
+
         drain(loads_in.at[pl.ds(0, GROUP - 1)], loads_recv)
         plane_loads[...] = jnp.sum(loads_in[...], axis=0)
         all_loads[k, z] = plane_loads[...]
@@ -265,7 +301,9 @@
         for face in range(4):
             weighted_copies[face].wait_recv()
             dual[rows(face), :] = 0.5 * difference(weighted[rows(face), :], weighted_in[rows(face), :], face)
-        local[...] = dot(neumann_own[...], dual[...].astype(BF16))
+            if face == 1:
+                local[...] = dot(neumann_own[:, 0:384], dual[0:384, :].astype(BF16))
+        local[...] += dot(neumann_own[:, 384:768], dual[384:768, :].astype(BF16))
         for face in range(4):
             weighted_copies[face].wait_send()
         third_sum = jnp.sum(dual[...] * local[...], axis=0, keepdims=True)
@@ -389,19 +427,24 @@
     lax.fori_loop(0, ITERS, iteration, 0)
     update()
 
+
+def restore(face_map, solved, residual, x_out, r_out, perms):
+    one_hots(face_map, perms)
     for value, out in ((solved, x_out), (residual, r_out)):
         out[0, 0:128, :] = value[0:128, :]
         out[0, 384:512, :] = value[384:512, :]
         for i in range(2):
-            out[0, windows[i], :] = permuted(perms[i].astype(F32).T.astype(BF16), value[windows[i], :])
+            out[0, WINDOWS[i], :] = permuted(perms[i].astype(F32).T.astype(BF16), value[WINDOWS[i], :])
 
 
 def body(source, neumann, dirichlet, coupling, corner_map, face_map, coarse_inverse):
     field = pltpu.VMEM((M, K), F32)
     square = pltpu.VMEM((M, M), BF16)
-    dma, one = pltpu.SemaphoreType.DMA, pltpu.SemaphoreType.DMA(())
+    plain, dma, one = pltpu.SemaphoreType.REGULAR, pltpu.SemaphoreType.DMA, pltpu.SemaphoreType.DMA(())
     scratch = [
-        field, field, field, field, field, field, field,
+        pltpu.VMEM((1, 4, M), F32), pltpu.VMEM((1, 4), jnp.int32), pltpu.VMEM((1, 2, FACE), jnp.int32),
+        pltpu.VMEM((129, 516), F32),
+        field, field, field, field, field,
         field, field,
         pltpu.VMEM((4, FACE // 2, 128), F32), pltpu.VMEM((4, FACE // 2, 128), F32), pltpu.VMEM((M, 128), F32),
         pltpu.VMEM((2, 256, 256), BF16), pltpu.VMEM((M + 128, M), BF16), square, square, square,
@@ -413,20 +456,30 @@
         pltpu.VMEM((8, 128), F32), pltpu.VMEM((ITERS, NZ, 8, 128), F32),
         pltpu.VMEM((8, 128), F32), pltpu.VMEM((ITERS, NZ, 8, 128), F32),
         pltpu.VMEM((16, 128), F32), pltpu.VMEM((GROUP, 16, 128), F32),
-        dma((3,)), dma((4,)), dma((4,)), dma((4,)), dma((4,)), dma((4,)), dma((4,)),
+        plain, plain, plain,
+        dma((7,)), dma((4,)), dma((4,)), dma((4,)), dma((4,)), dma((4,)), dma((4,)),
         dma((3,)), dma((3,)), dma((3,)), dma((3,)),
         one, one, one, dma((ITERS,)), one, dma((ITERS,)), one, one,
     ]
     vmem, hbm = pl.BlockSpec(memory_space=pltpu.VMEM), pl.BlockSpec(memory_space=pl.ANY)
-    return pl.pallas_call(
+    solved, residual = pl.pallas_call(
         kernel,
-        out_shape=(jax.ShapeDtypeStruct((1, M, K), F32), jax.ShapeDtypeStruct((1, M, K), F32)),
-        in_specs=[hbm, hbm, hbm, vmem, pl.BlockSpec(memory_space=pltpu.SMEM), vmem, vmem],
+        out_shape=(jax.ShapeDtypeStruct((M, K), F32), jax.ShapeDtypeStruct((M, K), F32)),
+        in_specs=[hbm] * 7,
         out_specs=(vmem, vmem),
         scratch_shapes=scratch,
         compiler_params=pltpu.CompilerParams(collective_id=0, has_side_effects=True, vmem_limit_bytes=62 * 2**20),
         cost_estimate=pl.CostEstimate(flops=3 * 4 * M * M * K, bytes_accessed=6 * 10**6, transcendentals=0),
     )(source, neumann, dirichlet, coupling, corner_map, face_map, coarse_inverse)
+    out = jax.ShapeDtypeStruct((1, M, K), F32)
+    return pl.pallas_call(
+        restore,
+        out_shape=(out, out),
+        in_specs=[vmem] * 3,
+        out_specs=(vmem, vmem),
+        scratch_shapes=[pltpu.VMEM((2, 256, 256), BF16)],
+        compiler_params=pltpu.CompilerParams(vmem_limit_bytes=63 * 2**20),
+    )(face_map, solved, residual)
 
 
 def solution(mesh):

time: 99.2 us -> 95 us (0.958)
  local copies, waits for them, and re-layouts: 3.02 us -> 0 us
  Pallas kernels: 95.3 us -> 94.2 us
    unnamed x4 -> x0, local copies, waits for them, and re-layouts: 3.02 us -> none
    pallas_call x1 -> x2, Pallas kernels: 95.3 us -> 94.2 us  [the longest x1 91 us: body(): pl.pallas_call(kernel, out_shape=(jax.ShapeDtypeStruct((M, K), F32), jax....]
where the time goes in v3:
time: 95 us; the launch traced here: 94.8 us
  Pallas kernels  94.2 us (99%)
    pallas_call x1, Pallas kernels, body(): pl.pallas_call(kernel, out_shape=(jax.ShapeDtypeStruct((M, K), F32), jax....  91 us
    pallas_call x1, Pallas kernels, body(): pl.pallas_call(restore, out_shape=(out, out), in_specs=[vmem] * 3, out_sp...  3.15 us

profile of v3, /device:TPU:1, one launch (start us, length us, event | category | flops | bytes accessed | tf_op | source)
XLA Modules:
  0.0 94.8 jit_solution(13074324697070577346)
XLA Ops:
  0.6 91.0 %shard_map.86 = (f32[768,256]{1,0:T(8,128)}, f32[768,256]{1,0:T(8,128)}) custom-call(f32[1,768,256]{2,1,0:T(8,128)} %source.1, bf16[1,768,768]{2,1,0:T(8,128)(2,1)} %neumann.1, bf16[1,768,768]{2,1,0:T(8,128)(2,1)} %dirichlet.1, f32[1,4,768]{2,1,0:T(4,128)} %coupling_in.1, s32[1,4]{1,0:T(1,128)} %corner_map_in.1, s32[1,2,192]{2,1,0:T(2,128)} %face_map.1, ...), custom_call_target="tpu_custom_call" | custom-call | flops 1811939328 | bytes 6000000 | tf_op jit(solution)/shard_map/pallas_call | solution.py:465
  91.7 3.2 %shard_map.87 = (f32[1,768,256]{2,1,0:T(8,128)}, f32[1,768,256]{2,1,0:T(8,128)}) custom-call(s32[1,2,192]{2,1,0:T(2,128)} %face_map.1, f32[768,256]{1,0:T(8,128)} %get-tuple-element.4.solved, f32[768,256]{1,0:T(8,128)} %get-tuple-element.5.residual), custom_call_target="tpu_custom_call" | custom-call | tf_op jit(solution)/shard_map/pallas_call | solution.py:475

commit v4 on v3

--- a/solution.py
+++ b/solution.py
@@ -21,6 +21,7 @@
 BASE = NX * PLANE
 USED = NX * (PLANE + 3)
 WIDE = 640
+PACK = FACE // 8
 
 
 def hops(step):
@@ -165,13 +166,12 @@
     frame[...] = scattered.T
     for i in range(2):
         frame[WINDOWS[i], :] = permuted(perms[i], frame[WINDOWS[i], :])
+    first_lane = NX * place + NX
     for face in range(4):
-        value = frame[rows(face), :]
-        if face == 0:
-            value = jnp.where(place == 0, pltpu.roll(value, BASE, 1), value)
-        if face == 1:
-            value = jnp.where(place == PLANE - 1, pltpu.roll(value, 128 - BASE, 1), value)
-        corner_out[face] = value[: FACE // 2] + pltpu.roll(value[FACE // 2 :], 64, 1)
+        value = pltpu.roll(frame[rows(face), :], 128 - first_lane, 1)
+        corner_out[face] = sum(
+            pltpu.roll(value[PACK * i : PACK * (i + 1)], 16 * i, 1) if i else value[0:PACK] for i in range(8)
+        )
 
     fetches[3].wait()
     for i in range(2):
@@ -222,13 +222,14 @@
     pl.semaphore_wait(near_sem, 2)
     greet(far_sem, [plane_at(4), plane_at(-4)])
 
-    low_lane = lax.broadcasted_iota(jnp.int32, (FACE // 2, 128), 1) < 64
-    for face in range(4):
+    in_use = lax.broadcasted_iota(jnp.int32, (PACK, 128), 1) < 8
+    for face, shift in zip(range(4), (-NX, NX, 0, 0)):
         corners[face].wait_recv()
         packed = corner_in[face]
         theirs = jnp.concatenate(
-            [jnp.where(low_lane, packed, 0.0), jnp.where(low_lane, pltpu.roll(packed, 64, 1), 0.0)], axis=0
-        )
+            [jnp.where(in_use, pltpu.roll(packed, 128 - 16 * i, 1) if i else packed, 0.0) for i in range(8)], axis=0
+        )
+        theirs = pltpu.roll(theirs, first_lane + shift, 1)
         frame[rows(face), :] = difference(frame[rows(face), :], theirs, face)
     jumped = frame[...]
     high = rounded(jumped)
@@ -446,7 +447,7 @@
         pltpu.VMEM((129, 516), F32),
         field, field, field, field, field,
         field, field,
-        pltpu.VMEM((4, FACE // 2, 128), F32), pltpu.VMEM((4, FACE // 2, 128), F32), pltpu.VMEM((M, 128), F32),
+        pltpu.VMEM((4, PACK, 128), F32), pltpu.VMEM((4, PACK, 128), F32), pltpu.VMEM((M, 128), F32),
         pltpu.VMEM((2, 256, 256), BF16), pltpu.VMEM((M + 128, M), BF16), square, square, square,
         pltpu.VMEM((M, 256), BF16),
         pltpu.VMEM((NX, 144, 516), F32), pltpu.VMEM((WIDE, WIDE), F32),

time: 95 us -> 94.2 us (level)
  no operation moved by 1% of the time
where the time goes in v4:
time: 94.2 us; the launch traced here: 94 us
  Pallas kernels  93.4 us (99%)
    pallas_call x1, Pallas kernels, body(): pl.pallas_call(kernel, out_shape=(jax.ShapeDtypeStruct((M, K), F32), jax....  90.2 us
    pallas_call x1, Pallas kernels, body(): pl.pallas_call(restore, out_shape=(out, out), in_specs=[vmem] * 3, out_sp...  3.15 us

profile of v4, /device:TPU:1, one launch (start us, length us, event | category | flops | bytes accessed | tf_op | source)
XLA Modules:
  0.0 94.0 jit_solution(7515830037196323646)
XLA Ops:
  0.6 90.2 %shard_map.86 = (f32[768,256]{1,0:T(8,128)}, f32[768,256]{1,0:T(8,128)}) custom-call(f32[1,768,256]{2,1,0:T(8,128)} %source.1, bf16[1,768,768]{2,1,0:T(8,128)(2,1)} %neumann.1, bf16[1,768,768]{2,1,0:T(8,128)(2,1)} %dirichlet.1, f32[1,4,768]{2,1,0:T(4,128)} %coupling_in.1, s32[1,4]{1,0:T(1,128)} %corner_map_in.1, s32[1,2,192]{2,1,0:T(2,128)} %face_map.1, ...), custom_call_target="tpu_custom_call" | custom-call | flops 1811939328 | bytes 6000000 | tf_op jit(solution)/shard_map/pallas_call | solution.py:466
  90.9 3.1 %shard_map.87 = (f32[1,768,256]{2,1,0:T(8,128)}, f32[1,768,256]{2,1,0:T(8,128)}) custom-call(s32[1,2,192]{2,1,0:T(2,128)} %face_map.1, f32[768,256]{1,0:T(8,128)} %get-tuple-element.4.solved, f32[768,256]{1,0:T(8,128)} %get-tuple-element.5.residual), custom_call_target="tpu_custom_call" | custom-call | tf_op jit(solution)/shard_map/pallas_call | solution.py:476

commit v5 on v4

--- a/solution.py
+++ b/solution.py
@@ -68,8 +68,8 @@
 
 def kernel(
     source, neumann, dirichlet, coupling_in, corner_map_in, face_map_in, coarse_inverse_in,
-    solved, residual,
-    coupling, corner_map, face_map, coarse_inverse, search, image, weighted, dual, local,
+    solved_out, residual_out,
+    solved, residual, coupling, corner_map, face_map, coarse_inverse, search, image, weighted, dual, local,
     weighted_in, local_in, corner_out, corner_in, frame,
     perms, dirichlet_all, neumann_own, raw_dirichlet, raw_neumann, spread,
     blocks, assembled, inverse_high, inverse_low, shifted, scalars,
@@ -426,7 +426,15 @@
         return carry
 
     lax.fori_loop(0, ITERS, iteration, 0)
+    results = [
+        pltpu.make_async_copy(residual, residual_out, fetch_sem.at[7]),
+        pltpu.make_async_copy(solved, solved_out, fetch_sem.at[8]),
+    ]
+    results[0].start()
     update()
+    results[1].start()
+    for result in results:
+        result.wait()
 
 
 def restore(face_map, solved, residual, x_out, r_out, perms):
@@ -443,7 +451,7 @@
     square = pltpu.VMEM((M, M), BF16)
     plain, dma, one = pltpu.SemaphoreType.REGULAR, pltpu.SemaphoreType.DMA, pltpu.SemaphoreType.DMA(())
     scratch = [
-        pltpu.VMEM((1, 4, M), F32), pltpu.VMEM((1, 4), jnp.int32), pltpu.VMEM((1, 2, FACE), jnp.int32),
+        field, field, pltpu.VMEM((1, 4, M), F32), pltpu.VMEM((1, 4), jnp.int32), pltpu.VMEM((1, 2, FACE), jnp.int32),
         pltpu.VMEM((129, 516), F32),
         field, field, field, field, field,
         field, field,
@@ -458,7 +466,7 @@
         pltpu.VMEM((8, 128), F32), pltpu.VMEM((ITERS, NZ, 8, 128), F32),
         pltpu.VMEM((16, 128), F32), pltpu.VMEM((GROUP, 16, 128), F32),
         plain, plain, plain,
-        dma((7,)), dma((4,)), dma((4,)), dma((4,)), dma((4,)), dma((4,)), dma((4,)),
+        dma((9,)), dma((4,)), dma((4,)), dma((4,)), dma((4,)), dma((4,)), dma((4,)),
         dma((3,)), dma((3,)), dma((3,)), dma((3,)),
         one, one, one, dma((ITERS,)), one, dma((ITERS,)), one, one,
     ]
@@ -467,7 +475,7 @@
         kernel,
         out_shape=(jax.ShapeDtypeStruct((M, K), F32), jax.ShapeDtypeStruct((M, K), F32)),
         in_specs=[hbm] * 7,
-        out_specs=(vmem, vmem),
+        out_specs=(hbm, hbm),
         scratch_shapes=scratch,
         compiler_params=pltpu.CompilerParams(collective_id=0, has_side_effects=True, vmem_limit_bytes=62 * 2**20),
         cost_estimate=pl.CostEstimate(flops=3 * 4 * M * M * K, bytes_accessed=6 * 10**6, transcendentals=0),

time: 94.2 us -> 94.2 us (level)
  no operation moved by 1% of the time
where the time goes in v5:
time: 94.2 us; the launch traced here: 94 us
  Pallas kernels  93.4 us (99%)
    pallas_call x1, Pallas kernels, body(): pl.pallas_call(kernel, out_shape=(jax.ShapeDtypeStruct((M, K), F32), jax....  90.2 us
    pallas_call x1, Pallas kernels, body(): pl.pallas_call(restore, out_shape=(out, out), in_specs=[vmem] * 3, out_sp...  3.15 us

profile of v5, /device:TPU:1, one launch (start us, length us, event | category | flops | bytes accessed | tf_op | source)
XLA Modules:
  0.0 94.0 jit_solution(11466323758449089078)
XLA Ops:
  0.6 90.2 %shard_map.86 = (f32[768,256]{1,0:T(8,128)}, f32[768,256]{1,0:T(8,128)}) custom-call(f32[1,768,256]{2,1,0:T(8,128)} %source.1, bf16[1,768,768]{2,1,0:T(8,128)(2,1)} %neumann.1, bf16[1,768,768]{2,1,0:T(8,128)(2,1)} %dirichlet.1, f32[1,4,768]{2,1,0:T(4,128)} %coupling_in.1, s32[1,4]{1,0:T(1,128)} %corner_map_in.1, s32[1,2,192]{2,1,0:T(2,128)} %face_map.1, ...), custom_call_target="tpu_custom_call" | custom-call | flops 1811939328 | bytes 6000000 | tf_op jit(solution)/shard_map/pallas_call | solution.py:474
  90.9 3.2 %shard_map.87 = (f32[1,768,256]{2,1,0:T(8,128)}, f32[1,768,256]{2,1,0:T(8,128)}) custom-call(s32[1,2,192]{2,1,0:T(2,128)} %face_map.1, f32[768,256]{1,0:T(8,128)} %get-tuple-element.4.solved, f32[768,256]{1,0:T(8,128)} %get-tuple-element.5.residual), custom_call_target="tpu_custom_call" | custom-call | tf_op jit(solution)/shard_map/pallas_call | solution.py:484
